TPU v7x, 32 devices: a whole 2x2x4 slice. The times are simulated.
32 devices in a mesh: dp: 4 (over y, x), tensor: 8 (over z, core).
Axes of the slice: x: 2, y: 2, z: 4, core: 2. Of those that a mesh axis runs over, the one named last changes fastest.
Arguments:
- grad_out: bfloat16 [64, 8192], P('dp'), may hold values from -6 to 6
- gate_act: bfloat16 [64, 1408], P('dp', 'tensor'), may hold values from -6 to 6
- up_act: bfloat16 [64, 1408], P('dp', 'tensor'), may hold values from -6 to 6
- w_gate: bfloat16 [1408, 8192], P('tensor'), may hold values from -0.0625 to 0.0625
- w_up: bfloat16 [1408, 8192], P('tensor'), may hold values from -0.0625 to 0.0625
- w_down: bfloat16 [1408, 8192], P('tensor'), may hold values from -0.15625 to 0.15625
Outputs:
- input_grad: bfloat16 [64, 8192], P(('dp', 'tensor'))
- down_grad: bfloat16 [1408, 8192], P('tensor', 'dp')
All inputs are finite; a program needn't handle non-finite values.
Results may differ from a plain program's by a relative error of at most 0.014.
Values may be sent and summed in bfloat16 or wider, within the bound.
A program may use at most 64 MiB of HBM per device.

v0:
```python
import jax
import jax.numpy as jnp
from jax import lax
from jax.sharding import PartitionSpec as P


def local(grad_out, gate_act, up_act, w_gate, w_up, w_down):
    gate = gate_act.astype(jnp.float32)
    up = up_act.astype(jnp.float32)
    sig = jax.nn.sigmoid(gate)
    silu = gate * sig
    hidden = (silu * up).astype(jnp.bfloat16)
    hidden_grad = lax.dot_general(
        grad_out, w_down, (((1,), (1,)), ((), ())), preferred_element_type=jnp.float32
    )
    gate_grad = (hidden_grad * up * sig * (1.0 + gate * (1.0 - sig))).astype(jnp.bfloat16)
    up_grad = (hidden_grad * silu).astype(jnp.bfloat16)
    full_terms = jnp.dot(gate_grad, w_gate, preferred_element_type=jnp.float32) + jnp.dot(
        up_grad, w_up, preferred_element_type=jnp.float32
    )
    summed = lax.psum_scatter(full_terms, "tensor", scatter_dimension=0, tiled=True)
    input_grad = summed.astype(jnp.bfloat16)
    partial_sum = lax.dot_general(
        hidden, grad_out, (((0,), (0,)), ((), ())), preferred_element_type=jnp.float32
    )
    down_grad = lax.psum_scatter(
        partial_sum.astype(jnp.bfloat16), "dp", scatter_dimension=1, tiled=True
    )
    return (input_grad, down_grad)


def solution(mesh):
    placed = (
        P("dp", None),
        P("dp", "tensor"),
        P("dp", "tensor"),
        P("tensor", None),
        P("tensor", None),
        P("tensor", None),
    )
    return jax.shard_map(
        local,
        mesh=mesh,
        in_specs=placed,
        out_specs=(P(("dp", "tensor"), None), P("tensor", "dp")),
        check_vma=False,
    )
```

profile of v0, /device:TPU:0, one launch (start us, length us, event | category | flops | bytes accessed | tf_op | source)
XLA Modules:
  0.0 63.0 jit_solution(11482301627427257563)
XLA Ops:
  7.2 0.0 copy-start
  7.2 0.0 copy-start.2
  7.2 0.0 reduce-scatter.2.cloned.1.call-start
  7.2 3.7 %convolution_convert_fusion = bf16[176,8192]{1,0:T(8,128)(2,1)} fusion(bf16[16,8192]{1,0:T(8,128)(2,1)} %param.6, bf16[16,176]{1,0:T(8,128)(2,1)} %param.8, bf16[16,176]{1,0:T(8,128)(2,1)} %param.7), kind=kOutput, calls=%fused_computation | convolution fusion | flops 47601664 | bytes 3156992 | tf_op jit(solution)/shard_map/dot_general | solution.py:23
  10.9 0.0 copy-start.3
  10.9 0.0 copy-start.4
  10.9 0.0 reduce-scatter.2.cloned.1.call-update
  10.9 0.0 copy-done.2
  11.0 0.0 copy-start.1
  11.0 2.8 %fusion.15 = f32[16,176]{1,0:T(8,128)S(1)} fusion(bf16[16,8192]{1,0:T(8,128)(2,1)S(1)} %copy-done.2, bf16[176,8192]{1,0:T(8,128)(2,1)} %param.11), kind=kOutput, calls=%fused_computation.22 | convolution fusion | flops 46137344 | bytes 3156992 | tf_op jit(solution)/shard_map/dot_general | solution.py:13
  13.8 0.0 copy-done
  13.8 0.0 copy-done.3
  13.8 0.0 copy-done.4
  13.8 0.0 copy-start.5
  13.8 0.5 fusion.9
  14.3 0.0 copy-done.1
  14.3 0.5 convolution_add_fusion
  14.8 0.0 copy-done.5
  14.8 0.6 dynamic-slice
  16.1 38.0 %all-reduce.2 = bf16[16,8192]{1,0:T(8,128)(2,1)} all-reduce(f32[16,8192]{1,0:T(8,128)S(1)} %convolution_add_fusion), channel_id=2, replica_groups=mesh['dp'=4,'tensor'=8] {'tensor'}, use_global_device_ids=true, to_apply=%region_0.0.clone | all-reduce | flops 131072 | bytes 786432
  54.1 1.6 %dynamic-slice_convert_fusion = bf16[2,8192]{1,0:T(2,128)(2,1)} fusion(bf16[16,8192]{1,0:T(8,128)(2,1)} %all-reduce.2, u32[]{:T(128)S(6)} %multiply.1), kind=kLoop, calls=%fused_computation.2 | loop fusion | bytes 65540 | tf_op jit(solution)/shard_map/convert_element_type | solution.py:22
  55.6 0.5 reduce-scatter.2.cloned.1.call-done
Async XLA Ops:
  7.2 6.6 %copy-start = (bf16[176,8192]{1,0:T(8,128)(2,1)S(1)}, bf16[176,8192]{1,0:T(8,128)(2,1)}, u32[]{:S(2)}) copy-start(bf16[176,8192]{1,0:T(8,128)(2,1)} %param.9) | copy-start | bytes 8650756
  7.2 3.8 %copy-start.2 = (bf16[16,8192]{1,0:T(8,128)(2,1)S(1)}, bf16[16,8192]{1,0:T(8,128)(2,1)}, u32[]{:S(2)}) copy-start(bf16[16,8192]{1,0:T(8,128)(2,1)} %param.6) | copy-start | bytes 786436
  7.2 48.9 %reduce-scatter.2.cloned.1.call-start = ((), (), s32[]{:S(2)}) async-start(), calls=%async_computation.1 | async-start | bytes 3604480 | tf_op jit(solution)/shard_map/reduce_scatter | solution.py:26
  10.9 2.9 %copy-start.3 = (bf16[16,176]{1,0:T(8,128)(2,1)S(1)}, bf16[16,176]{1,0:T(8,128)(2,1)}, u32[]{:S(2)}) copy-start(bf16[16,176]{1,0:T(8,128)(2,1)} %param.7) | copy-start | bytes 16900
  10.9 2.9 %copy-start.4 = (bf16[16,176]{1,0:T(8,128)(2,1)S(1)}, bf16[16,176]{1,0:T(8,128)(2,1)}, u32[]{:S(2)}) copy-start(bf16[16,176]{1,0:T(8,128)(2,1)} %param.8) | copy-start | bytes 16900
  11.0 3.4 %copy-start.1 = (bf16[176,8192]{1,0:T(8,128)(2,1)S(1)}, bf16[176,8192]{1,0:T(8,128)(2,1)}, u32[]{:S(2)}) copy-start(bf16[176,8192]{1,0:T(8,128)(2,1)} %param.10) | copy-start | bytes 8650756
  13.8 1.0 %copy-start.5 = (u32[32]{0:T(128)S(1)}, u32[32]{0:T(128)}, u32[]{:S(2)}) copy-start(u32[32]{0:T(128)} %constant.4) | copy-start | bytes 388
Sparse Core Ops, SparseCore 0:
  11.6 44.4 reduce-scatter.1
where the time goes:
time: 63.2 us; the launch traced here: 63 us
  blocking collectives  38 us (60%)
  between operations  14.7 us (23%)
  matrix products  7.5 us (12%)
  local copies, waits for them, and re-layouts  2.2 us (3%)
    unnamed x1, blocking collectives  38 us
    dot_general x1, matrix products, local(): lax.dot_general(hidden, grad_out, (((0,), (0,)), ((), ())), preferred_ele...  3.68 us
    dot_general x1, matrix products, local(): lax.dot_general(grad_out, w_down, (((1,), (1,)), ((), ())), preferred_ele...  2.81 us
    convert_element_type x1, local copies, waits for them, and re-layouts, local(): input_grad = summed.astype(jnp.bfloat16)  1.56 us
  transfers between devices with their start and end apart: 1, of which 1 were waited for; matrix products, arithmetic and copies ran while one was open for 9% of the time, Pallas kernels for 0%

commit v1 on v0

v1 whole, which is shorter than its diff:
```python
import functools

import jax
import jax.numpy as jnp
from jax import lax
from jax.experimental import pallas as pl
from jax.experimental.pallas import tpu as pltpu
from jax.sharding import PartitionSpec as P

MESH = pl.DeviceIdType.MESH
PARTS = 4
F32 = jnp.float32
BF16 = jnp.bfloat16


def kernel(n_dp, n_t, g_hbm, gate_hbm, up_hbm, wg_hbm, wu_hbm, wd_hbm, ig_hbm, dg_hbm,
           g, gate_v, up_v, wg, wu, wd, g_all, h_all, to_pair, from_pair, mine, to_chips, from_chips,
           ig, dg, in_sem, wg_sem, wu_sem, wd_sem, own_sem, gs_sem, gr_sem, hs_sem, hr_sem,
           ps_sem, pr_sem, zs_sem, zr_sem, out_sem):
    tokens, width = g.shape
    units = gate_v.shape[1]
    chips = n_t // 2
    rows = tokens // n_t
    half = tokens // 2
    piece = width // PARTS
    cut = width // n_dp
    i = lax.axis_index("dp")
    t = lax.axis_index("tensor")
    chip, core = t // 2, lax.rem(t, 2)
    pair = t + 1 - 2 * core

    def chip_at(q):
        return 2 * lax.rem(chip + q, chips) + core

    def row_at(q):
        return lax.rem(i + q, n_dp)

    loads = [
        pltpu.make_async_copy(gate_hbm, gate_v, in_sem.at[0]),
        pltpu.make_async_copy(up_hbm, up_v, in_sem.at[1]),
        pltpu.make_async_copy(g_hbm, g, in_sem.at[2]),
    ]
    own = pltpu.make_async_copy(
        g_hbm.at[:, pl.ds(pl.multiple_of(i * cut, cut), cut)], g_all.at[pl.ds(0, tokens)], own_sem
    )
    weights = []
    for source, target, sem in ((wd_hbm, wd, wd_sem), (wg_hbm, wg, wg_sem), (wu_hbm, wu, wu_sem)):
        weights.append([
            pltpu.make_async_copy(source.at[:, pl.ds(k * piece, piece)], target.at[k], sem.at[k])
            for k in range(PARTS)
        ])
    wd_loads, wg_loads, wu_loads = weights
    for copy in loads + wd_loads:
        copy.start()

    barrier = pltpu.get_barrier_semaphore()
    pl.semaphore_signal(barrier, inc=1, device_id=(i, pair), device_id_type=MESH)
    for q in range(1, chips):
        pl.semaphore_signal(barrier, inc=1, device_id=(i, chip_at(q)), device_id_type=MESH)
    for q in range(1, n_dp):
        pl.semaphore_signal(barrier, inc=1, device_id=(row_at(q), t), device_id_type=MESH)

    for k in range(PARTS):
        wg_loads[k].start()
        wu_loads[k].start()
    own.start()

    loads[0].wait()
    loads[1].wait()
    gate = gate_v[...].astype(F32)
    up = up_v[...].astype(F32)
    sig = jax.nn.sigmoid(gate)
    silu = gate * sig
    h_all[pl.ds(0, tokens), :] = (silu * up).astype(BF16)

    pl.semaphore_wait(barrier, chips + n_dp - 1)
    gathers = []
    for q in range(1, n_dp):
        there = row_at(q)
        gathers.append(pltpu.make_async_remote_copy(
            src_ref=g_hbm.at[:, pl.ds(pl.multiple_of(there * cut, cut), cut)],
            dst_ref=g_all.at[pl.ds(q * tokens, tokens)],
            send_sem=gs_sem.at[q - 1], recv_sem=gr_sem.at[q - 1],
            device_id=(there, t), device_id_type=MESH,
        ))
        gathers.append(pltpu.make_async_remote_copy(
            src_ref=h_all.at[pl.ds(0, tokens)],
            dst_ref=h_all.at[pl.ds(q * tokens, tokens)],
            send_sem=hs_sem.at[q - 1], recv_sem=hr_sem.at[q - 1],
            device_id=(there, t), device_id_type=MESH,
        ))
    for copy in gathers:
        copy.start()

    loads[2].wait()
    hg = jnp.zeros((tokens, units), F32)
    for k in range(PARTS):
        wd_loads[k].wait()
        hg = hg + lax.dot_general(
            g[:, k * piece:(k + 1) * piece], wd[k], (((1,), (1,)), ((), ())), preferred_element_type=F32
        )
    gg = (hg * up * sig * (1.0 + gate * (1.0 - sig))).astype(BF16)
    ug = (hg * silu).astype(BF16)

    place = lax.broadcasted_iota(jnp.int32, (tokens, tokens), 0)
    token = lax.broadcasted_iota(jnp.int32, (tokens, tokens), 1)
    ours = (place >= half).astype(jnp.int32)
    inner = place - ours * half
    hop = inner // rows
    side = jnp.where(ours == 1, core, 1 - core)
    at_chip = chip + hop
    at_chip = jnp.where(at_chip >= chips, at_chip - chips, at_chip)
    wanted = (2 * at_chip + side) * rows + (inner - hop * rows)
    order = (wanted == token).astype(F32).astype(BF16)
    gg = jnp.dot(order, gg, preferred_element_type=F32).astype(BF16)
    ug = jnp.dot(order, ug, preferred_element_type=F32).astype(BF16)

    pair_copies = [
        pltpu.make_async_remote_copy(
            src_ref=to_pair.at[k], dst_ref=from_pair.at[k],
            send_sem=ps_sem.at[k], recv_sem=pr_sem.at[k],
            device_id=(i, pair), device_id_type=MESH,
        )
        for k in range(PARTS)
    ]

    def produce(k):
        wg_loads[k].wait()
        wu_loads[k].wait()
        terms = jnp.dot(gg, wg[k], preferred_element_type=F32) + jnp.dot(ug, wu[k], preferred_element_type=F32)
        to_pair[k] = terms[:half]
        pair_copies[k].start()
        mine[k] = terms[half:]

    def forward(k):
        pair_copies[k].wait_recv()
        mine[k] = mine[k] + from_pair[k]
        for q in range(1, chips):
            to_chips[k, q - 1] = mine[k, q * rows:(q + 1) * rows, :].astype(BF16)
        for q in range(1, chips):
            pltpu.make_async_remote_copy(
                src_ref=to_chips.at[k, q - 1], dst_ref=from_chips.at[k, q - 1],
                send_sem=zs_sem.at[k], recv_sem=zr_sem.at[k],
                device_id=(i, chip_at(q)), device_id_type=MESH,
            ).start()

    for k in range(PARTS):
        produce(k)
        if k > 0:
            forward(k - 1)
    forward(PARTS - 1)

    for copy in gathers:
        copy.wait_recv()
    own.wait()
    dg[...] = lax.dot_general(
        h_all[...], g_all[...], (((0,), (0,)), ((), ())), preferred_element_type=F32
    ).astype(BF16)
    dg_store = pltpu.make_async_copy(dg, dg_hbm, out_sem.at[0])
    dg_store.start()

    for k in range(PARTS):
        pltpu.make_async_copy(from_chips.at[k], from_chips.at[k], zr_sem.at[k]).wait()
        total = mine[k, 0:rows, :]
        for q in range(1, chips):
            total = total + from_chips[k, q - 1].astype(F32)
        ig[:, k * piece:(k + 1) * piece] = total.astype(BF16)
    ig_store = pltpu.make_async_copy(ig, ig_hbm, out_sem.at[1])
    ig_store.start()

    for copy in gathers + pair_copies:
        copy.wait_send()
    for k in range(PARTS):
        pltpu.make_async_copy(to_chips.at[k], to_chips.at[k], zs_sem.at[k]).wait()
    dg_store.wait()
    ig_store.wait()


def local(n_dp, n_t, grad_out, gate_act, up_act, w_gate, w_up, w_down):
    tokens, width = grad_out.shape
    units = gate_act.shape[1]
    chips, rows, half = n_t // 2, tokens // n_t, tokens // 2
    piece, cut = width // PARTS, width // n_dp
    dma = pltpu.SemaphoreType.DMA
    anywhere = pl.BlockSpec(memory_space=pl.ANY)
    return pl.pallas_call(
        functools.partial(kernel, n_dp, n_t),
        out_shape=(
            jax.ShapeDtypeStruct((rows, width), BF16),
            jax.ShapeDtypeStruct((units, cut), BF16),
        ),
        in_specs=[anywhere] * 6,
        out_specs=(anywhere, anywhere),
        scratch_shapes=[
            pltpu.VMEM((tokens, width), BF16),
            pltpu.VMEM((tokens, units), BF16),
            pltpu.VMEM((tokens, units), BF16),
            pltpu.VMEM((PARTS, units, piece), BF16),
            pltpu.VMEM((PARTS, units, piece), BF16),
            pltpu.VMEM((PARTS, units, piece), BF16),
            pltpu.VMEM((n_dp * tokens, cut), BF16),
            pltpu.VMEM((n_dp * tokens, units), BF16),
            pltpu.VMEM((PARTS, half, piece), F32),
            pltpu.VMEM((PARTS, half, piece), F32),
            pltpu.VMEM((PARTS, half, piece), F32),
            pltpu.VMEM((PARTS, chips - 1, rows, piece), BF16),
            pltpu.VMEM((PARTS, chips - 1, rows, piece), BF16),
            pltpu.VMEM((rows, width), BF16),
            pltpu.VMEM((units, cut), BF16),
            dma((3,)),
            dma((PARTS,)),
            dma((PARTS,)),
            dma((PARTS,)),
            dma,
            dma((n_dp - 1,)),
            dma((n_dp - 1,)),
            dma((n_dp - 1,)),
            dma((n_dp - 1,)),
            dma((PARTS,)),
            dma((PARTS,)),
            dma((PARTS,)),
            dma((PARTS,)),
            dma((2,)),
        ],
        compiler_params=pltpu.CompilerParams(
            collective_id=0, has_side_effects=True, vmem_limit_bytes=56 * 1024 * 1024
        ),
        cost_estimate=pl.CostEstimate(
            flops=2 * tokens * units * width * 4, bytes_accessed=3 * 2 * units * width, transcendentals=tokens * units
        ),
    )(grad_out, gate_act, up_act, w_gate, w_up, w_down)


def solution(mesh):
    placed = (
        P("dp", None),
        P("dp", "tensor"),
        P("dp", "tensor"),
        P("tensor", None),
        P("tensor", None),
        P("tensor", None),
    )
    return jax.shard_map(
        functools.partial(local, mesh.shape["dp"], mesh.shape["tensor"]),
        mesh=mesh,
        in_specs=placed,
        out_specs=(P(("dp", "tensor"), None), P("tensor", "dp")),
        check_vma=False,
    )
```

time: 63.2 us -> 19.9 us (0.31)
  blocking collectives: 38 us -> 0 us
  Pallas kernels: 0 us -> 15.6 us
  between operations: 14.7 us -> 0.64 us
  matrix products: 7.5 us -> 0 us
  local copies, waits for them, and re-layouts: 2.2 us -> 3.44 us
    unnamed x1 -> x0, blocking collectives: 38 us -> none
    pallas_call x0 -> x1, Pallas kernels: none -> 15.6 us  [local(): pl.pallas_call(functools.partial(kernel, n_dp, n_t), out_shape=(jax.Shape...]
    dot_general x4 -> x0, matrix products: 7.5 us -> none  [the longest x1 3.68 us: local(): lax.dot_general(hidden, grad_out, (((0,), (0,)), ((), ())), preferred_ele...]
    unnamed x13 -> x2, local copies, waits for them, and re-layouts: 0.64 us -> 3.44 us
    convert_element_type x1 -> x0, local copies, waits for them, and re-layouts: 1.56 us -> none  [local(): input_grad = summed.astype(jnp.bfloat16)]
  transfers between devices with their start and end apart: 1 -> 0, of which waited for: 1 -> 0; matrix products, arithmetic and copies ran while one was open for 9% -> 0% of each run, Pallas kernels for 0% -> 0%
where the time goes in v1:
time: 19.9 us; the launch traced here: 19.7 us
  Pallas kernels  15.6 us (78%)
  local copies, waits for them, and re-layouts  3.44 us (17%)
  between operations  0.64 us (3%)
    pallas_call x1, Pallas kernels, local(): pl.pallas_call(functools.partial(kernel, n_dp, n_t), out_shape=(jax.Shape...  15.6 us
    unnamed x2, local copies, waits for them, and re-layouts  3.44 us

profile of v1, /device:TPU:0, one launch (start us, length us, event | category | flops | bytes accessed | tf_op | source)
XLA Modules:
  0.0 19.7 jit_solution(1717283632066169220)
XLA Ops:
  0.6 15.6 %shard_map.77 = (bf16[2,8192]{1,0:T(2,128)(2,1)}, bf16[176,2048]{1,0:T(8,128)(2,1)}) custom-call(bf16[16,8192]{1,0:T(8,128)(2,1)} %g_hbm.1, bf16[16,176]{1,0:T(8,128)(2,1)} %gate_hbm.1, bf16[16,176]{1,0:T(8,128)(2,1)} %up_hbm.1, bf16[176,8192]{1,0:T(8,128)(2,1)} %wg_hbm.1, bf16[176,8192]{1,0:T(8,128)(2,1)} %wu_hbm.1, bf16[176,8192]{1,0:T(8,128)(2,1)} %wd_hbm.1), custom_call_target="tpu_custom_call" | custom-call | flops 184549376 | bytes 8650752 | tf_op jit(solution)/shard_map/pallas_call | solution.py:186
  16.3 1.4 %copy.10 = bf16[2,8192]{1,0:T(2,128)(2,1)} copy(bf16[2,8192]{1,0:T(2,128)(2,1)} %get-tuple-element.4) | data formatting | bytes 65536
  17.6 2.0 %copy.11 = bf16[176,2048]{1,0:T(8,128)(2,1)} copy(bf16[176,2048]{1,0:T(8,128)(2,1)} %get-tuple-element.5) | data formatting | bytes 1441792

commit v2 on v1

--- a/solution.py
+++ b/solution.py
@@ -13,10 +13,10 @@
 BF16 = jnp.bfloat16
 
 
-def kernel(n_dp, n_t, g_hbm, gate_hbm, up_hbm, wg_hbm, wu_hbm, wd_hbm, ig_hbm, dg_hbm,
+def kernel(n_dp, n_t, g_hbm, gate_hbm, up_hbm, wg_hbm, wu_hbm, wd_hbm, ig, dg,
            g, gate_v, up_v, wg, wu, wd, g_all, h_all, to_pair, from_pair, mine, to_chips, from_chips,
-           ig, dg, in_sem, wg_sem, wu_sem, wd_sem, own_sem, gs_sem, gr_sem, hs_sem, hr_sem,
-           ps_sem, pr_sem, zs_sem, zr_sem, out_sem):
+           in_sem, wg_sem, wu_sem, wd_sem, own_sem, gs_sem, gr_sem, hs_sem, hr_sem,
+           ps_sem, pr_sem, zs_sem, zr_sem):
     tokens, width = g.shape
     units = gate_v.shape[1]
     chips = n_t // 2
@@ -156,8 +156,6 @@
     dg[...] = lax.dot_general(
         h_all[...], g_all[...], (((0,), (0,)), ((), ())), preferred_element_type=F32
     ).astype(BF16)
-    dg_store = pltpu.make_async_copy(dg, dg_hbm, out_sem.at[0])
-    dg_store.start()
 
     for k in range(PARTS):
         pltpu.make_async_copy(from_chips.at[k], from_chips.at[k], zr_sem.at[k]).wait()
@@ -165,15 +163,22 @@
         for q in range(1, chips):
             total = total + from_chips[k, q - 1].astype(F32)
         ig[:, k * piece:(k + 1) * piece] = total.astype(BF16)
-    ig_store = pltpu.make_async_copy(ig, ig_hbm, out_sem.at[1])
-    ig_store.start()
 
     for copy in gathers + pair_copies:
         copy.wait_send()
     for k in range(PARTS):
         pltpu.make_async_copy(to_chips.at[k], to_chips.at[k], zs_sem.at[k]).wait()
-    dg_store.wait()
-    ig_store.wait()
+
+
+def place_kernel(ig, dg, ig_hbm, dg_hbm, sem):
+    copies = [
+        pltpu.make_async_copy(dg, dg_hbm, sem.at[0]),
+        pltpu.make_async_copy(ig, ig_hbm, sem.at[1]),
+    ]
+    for copy in copies:
+        copy.start()
+    for copy in copies:
+        copy.wait()
 
 
 def local(n_dp, n_t, grad_out, gate_act, up_act, w_gate, w_up, w_down):
@@ -183,14 +188,14 @@
     piece, cut = width // PARTS, width // n_dp
     dma = pltpu.SemaphoreType.DMA
     anywhere = pl.BlockSpec(memory_space=pl.ANY)
-    return pl.pallas_call(
+    held = pl.pallas_call(
         functools.partial(kernel, n_dp, n_t),
         out_shape=(
-            jax.ShapeDtypeStruct((rows, width), BF16),
-            jax.ShapeDtypeStruct((units, cut), BF16),
+            pltpu.VMEM((rows, width), BF16),
+            pltpu.VMEM((units, cut), BF16),
         ),
         in_specs=[anywhere] * 6,
-        out_specs=(anywhere, anywhere),
+        out_specs=(pl.BlockSpec(memory_space=pltpu.VMEM),) * 2,
         scratch_shapes=[
             pltpu.VMEM((tokens, width), BF16),
             pltpu.VMEM((tokens, units), BF16),
@@ -205,8 +210,6 @@
             pltpu.VMEM((PARTS, half, piece), F32),
             pltpu.VMEM((PARTS, chips - 1, rows, piece), BF16),
             pltpu.VMEM((PARTS, chips - 1, rows, piece), BF16),
-            pltpu.VMEM((rows, width), BF16),
-            pltpu.VMEM((units, cut), BF16),
             dma((3,)),
             dma((PARTS,)),
             dma((PARTS,)),
@@ -220,7 +223,6 @@
             dma((PARTS,)),
             dma((PARTS,)),
             dma((PARTS,)),
-            dma((2,)),
         ],
         compiler_params=pltpu.CompilerParams(
             collective_id=0, has_side_effects=True, vmem_limit_bytes=56 * 1024 * 1024
@@ -229,6 +231,17 @@
             flops=2 * tokens * units * width * 4, bytes_accessed=3 * 2 * units * width, transcendentals=tokens * units
         ),
     )(grad_out, gate_act, up_act, w_gate, w_up, w_down)
+    held = [pltpu.with_memory_space_constraint(x, pltpu.VMEM) for x in held]
+    return pl.pallas_call(
+        place_kernel,
+        out_shape=(
+            jax.ShapeDtypeStruct((rows, width), BF16),
+            jax.ShapeDtypeStruct((units, cut), BF16),
+        ),
+        in_specs=[pl.BlockSpec(memory_space=pltpu.VMEM)] * 2,
+        out_specs=(anywhere, anywhere),
+        scratch_shapes=[dma((2,))],
+    )(*held)
 
 
 def solution(mesh):

time: 19.9 us -> 16.7 us (0.84)
  local copies, waits for them, and re-layouts: 3.44 us -> 0 us
  Pallas kernels: 15.6 us -> 15.9 us
    unnamed x2 -> x0, local copies, waits for them, and re-layouts: 3.44 us -> none
    pallas_call x1 -> x2, Pallas kernels: 15.6 us -> 15.9 us  [the longest x1 15 us: local(): pl.pallas_call(functools.partial(kernel, n_dp, n_t), out_shape=(pltpu.VME...]
where the time goes in v2:
time: 16.7 us; the launch traced here: 16.5 us
  Pallas kernels  15.9 us (95%)
  between operations  0.64 us (4%)
    pallas_call x1, Pallas kernels, local(): pl.pallas_call(functools.partial(kernel, n_dp, n_t), out_shape=(pltpu.VME...  15 us
    pallas_call x1, Pallas kernels, local(): pl.pallas_call(place_kernel, out_shape=(jax.ShapeDtypeStruct((rows, width...  0.88 us

profile of v2, /device:TPU:0, one launch (start us, length us, event | category | flops | bytes accessed | tf_op | source)
XLA Modules:
  0.0 16.5 jit_solution(17333941788189337387)
XLA Ops:
  0.6 15.0 %shard_map.77 = (bf16[2,8192]{1,0:T(2,128)(2,1)S(1)}, bf16[176,2048]{1,0:T(8,128)(2,1)S(1)}) custom-call(bf16[16,8192]{1,0:T(8,128)(2,1)} %g_hbm.1, bf16[16,176]{1,0:T(8,128)(2,1)} %gate_hbm.1, bf16[16,176]{1,0:T(8,128)(2,1)} %up_hbm.1, bf16[176,8192]{1,0:T(8,128)(2,1)} %wg_hbm.1, bf16[176,8192]{1,0:T(8,128)(2,1)} %wu_hbm.1, bf16[176,8192]{1,0:T(8,128)(2,1)} %wd_hbm.1), custom_call_target="tpu_custom_call" | custom-call | flops 184549376 | bytes 8650752 | tf_op jit(solution)/shard_map/pallas_call | solution.py:191
  15.6 0.9 %shard_map.78 = (bf16[2,8192]{1,0:T(2,128)(2,1)}, bf16[176,2048]{1,0:T(8,128)(2,1)}) custom-call(bf16[2,8192]{1,0:T(2,128)(2,1)S(1)} %get-tuple-element.4.ig, bf16[176,2048]{1,0:T(8,128)(2,1)S(1)} %get-tuple-element.5.dg), custom_call_target="tpu_custom_call" | custom-call | tf_op jit(solution)/shard_map/pallas_call | solution.py:235

commit v3 on v2

--- a/solution.py
+++ b/solution.py
@@ -8,7 +8,8 @@
 from jax.sharding import PartitionSpec as P
 
 MESH = pl.DeviceIdType.MESH
-PARTS = 4
+PARTS = 2
+STEPS = 4
 F32 = jnp.float32
 BF16 = jnp.bfloat16
 
@@ -23,6 +24,7 @@
     rows = tokens // n_t
     half = tokens // 2
     piece = width // PARTS
+    step = width // STEPS
     cut = width // n_dp
     i = lax.axis_index("dp")
     t = lax.axis_index("tensor")
@@ -44,10 +46,12 @@
         g_hbm.at[:, pl.ds(pl.multiple_of(i * cut, cut), cut)], g_all.at[pl.ds(0, tokens)], own_sem
     )
     weights = []
-    for source, target, sem in ((wd_hbm, wd, wd_sem), (wg_hbm, wg, wg_sem), (wu_hbm, wu, wu_sem)):
+    for source, target, sem, wide in (
+        (wd_hbm, wd, wd_sem, step), (wg_hbm, wg, wg_sem, piece), (wu_hbm, wu, wu_sem, piece)
+    ):
         weights.append([
-            pltpu.make_async_copy(source.at[:, pl.ds(k * piece, piece)], target.at[k], sem.at[k])
-            for k in range(PARTS)
+            pltpu.make_async_copy(source.at[:, pl.ds(k * wide, wide)], target.at[k], sem.at[k])
+            for k in range(width // wide)
         ])
     wd_loads, wg_loads, wu_loads = weights
     for copy in loads + wd_loads:
@@ -73,7 +77,22 @@
     silu = gate * sig
     h_all[pl.ds(0, tokens), :] = (silu * up).astype(BF16)
 
-    pl.semaphore_wait(barrier, chips + n_dp - 1)
+    place = lax.broadcasted_iota(jnp.int32, (tokens, tokens), 0)
+    token = lax.broadcasted_iota(jnp.int32, (tokens, tokens), 1)
+    ours = (place >= half).astype(jnp.int32)
+    inner = place - ours * half
+    hop = inner // rows
+    side = jnp.where(ours == 1, core, 1 - core)
+    at_chip = chip + hop
+    at_chip = jnp.where(at_chip >= chips, at_chip - chips, at_chip)
+    wanted = (2 * at_chip + side) * rows + (inner - hop * rows)
+    order = (wanted == token).astype(F32).astype(BF16)
+    gate = jnp.dot(order, gate_v[...], preferred_element_type=F32)
+    up = jnp.dot(order, up_v[...], preferred_element_type=F32)
+    sig = jax.nn.sigmoid(gate)
+    silu = gate * sig
+    gate_factor = up * sig * (1.0 + gate * (1.0 - sig))
+
     gathers = []
     for q in range(1, n_dp):
         there = row_at(q)
@@ -89,31 +108,28 @@
             send_sem=hs_sem.at[q - 1], recv_sem=hr_sem.at[q - 1],
             device_id=(there, t), device_id_type=MESH,
         ))
-    for copy in gathers:
-        copy.start()
 
     loads[2].wait()
-    hg = jnp.zeros((tokens, units), F32)
-    for k in range(PARTS):
+    for k in range(STEPS):
+        part = slice(k * step, (k + 1) * step)
+        g[:, part] = jnp.dot(order, g[:, part], preferred_element_type=F32).astype(BF16)
+    sums = [jnp.zeros((tokens, units), F32) for _ in range(4)]
+    for k in range(STEPS):
         wd_loads[k].wait()
-        hg = hg + lax.dot_general(
-            g[:, k * piece:(k + 1) * piece], wd[k], (((1,), (1,)), ((), ())), preferred_element_type=F32
-        )
-    gg = (hg * up * sig * (1.0 + gate * (1.0 - sig))).astype(BF16)
+        for n in range(4):
+            quarter = step // 4
+            sums[n] = sums[n] + lax.dot_general(
+                g[:, k * step + n * quarter:k * step + (n + 1) * quarter], wd[k, :, n * quarter:(n + 1) * quarter],
+                (((1,), (1,)), ((), ())), preferred_element_type=F32
+            )
+        if k == 1:
+            pl.semaphore_wait(barrier, chips + n_dp - 1)
+            for copy in gathers:
+                copy.start()
+    hg = (sums[0] + sums[1]) + (sums[2] + sums[3])
+
+    gg = (hg * gate_factor).astype(BF16)
     ug = (hg * silu).astype(BF16)
-
-    place = lax.broadcasted_iota(jnp.int32, (tokens, tokens), 0)
-    token = lax.broadcasted_iota(jnp.int32, (tokens, tokens), 1)
-    ours = (place >= half).astype(jnp.int32)
-    inner = place - ours * half
-    hop = inner // rows
-    side = jnp.where(ours == 1, core, 1 - core)
-    at_chip = chip + hop
-    at_chip = jnp.where(at_chip >= chips, at_chip - chips, at_chip)
-    wanted = (2 * at_chip + side) * rows + (inner - hop * rows)
-    order = (wanted == token).astype(F32).astype(BF16)
-    gg = jnp.dot(order, gg, preferred_element_type=F32).astype(BF16)
-    ug = jnp.dot(order, ug, preferred_element_type=F32).astype(BF16)
 
     pair_copies = [
         pltpu.make_async_remote_copy(
@@ -185,7 +201,7 @@
     tokens, width = grad_out.shape
     units = gate_act.shape[1]
     chips, rows, half = n_t // 2, tokens // n_t, tokens // 2
-    piece, cut = width // PARTS, width // n_dp
+    piece, step, cut = width // PARTS, width // STEPS, width // n_dp
     dma = pltpu.SemaphoreType.DMA
     anywhere = pl.BlockSpec(memory_space=pl.ANY)
     held = pl.pallas_call(
@@ -202,7 +218,7 @@
             pltpu.VMEM((tokens, units), BF16),
             pltpu.VMEM((PARTS, units, piece), BF16),
             pltpu.VMEM((PARTS, units, piece), BF16),
-            pltpu.VMEM((PARTS, units, piece), BF16),
+            pltpu.VMEM((STEPS, units, step), BF16),
             pltpu.VMEM((n_dp * tokens, cut), BF16),
             pltpu.VMEM((n_dp * tokens, units), BF16),
             pltpu.VMEM((PARTS, half, piece), F32),
@@ -213,7 +229,7 @@
             dma((3,)),
             dma((PARTS,)),
             dma((PARTS,)),
-            dma((PARTS,)),
+            dma((STEPS,)),
             dma,
             dma((n_dp - 1,)),
             dma((n_dp - 1,)),

time: 16.7 us -> 15.3 us (0.916)
  Pallas kernels: 15.9 us -> 14.5 us
    pallas_call x1, Pallas kernels: 15 us -> 13.7 us  [local(): pl.pallas_call(functools.partial(kernel, n_dp, n_t), out_shape=(pltpu.VME...]
where the time goes in v3:
time: 15.3 us; the launch traced here: 15.2 us
  Pallas kernels  14.5 us (95%)
  between operations  0.64 us (4%)
    pallas_call x1, Pallas kernels, local(): pl.pallas_call(functools.partial(kernel, n_dp, n_t), out_shape=(pltpu.VME...  13.7 us
    pallas_call x1, Pallas kernels, local(): pl.pallas_call(place_kernel, out_shape=(jax.ShapeDtypeStruct((rows, width...  0.88 us

profile of v3, /device:TPU:0, one launch (start us, length us, event | category | flops | bytes accessed | tf_op | source)
XLA Modules:
  0.0 15.2 jit_solution(2777632301326624946)
XLA Ops:
  0.6 13.7 %shard_map.77 = (bf16[2,8192]{1,0:T(2,128)(2,1)S(1)}, bf16[176,2048]{1,0:T(8,128)(2,1)S(1)}) custom-call(bf16[16,8192]{1,0:T(8,128)(2,1)} %g_hbm.1, bf16[16,176]{1,0:T(8,128)(2,1)} %gate_hbm.1, bf16[16,176]{1,0:T(8,128)(2,1)} %up_hbm.1, bf16[176,8192]{1,0:T(8,128)(2,1)} %wg_hbm.1, bf16[176,8192]{1,0:T(8,128)(2,1)} %wu_hbm.1, bf16[176,8192]{1,0:T(8,128)(2,1)} %wd_hbm.1), custom_call_target="tpu_custom_call" | custom-call | flops 184549376 | bytes 8650752 | tf_op jit(solution)/shard_map/pallas_call | solution.py:207
  14.3 0.9 %shard_map.78 = (bf16[2,8192]{1,0:T(2,128)(2,1)}, bf16[176,2048]{1,0:T(8,128)(2,1)}) custom-call(bf16[2,8192]{1,0:T(2,128)(2,1)S(1)} %get-tuple-element.4.ig, bf16[176,2048]{1,0:T(8,128)(2,1)S(1)} %get-tuple-element.5.dg), custom_call_target="tpu_custom_call" | custom-call | tf_op jit(solution)/shard_map/pallas_call | solution.py:251

commit v4 on v3

--- a/solution.py
+++ b/solution.py
@@ -150,10 +150,9 @@
 
     def forward(k):
         pair_copies[k].wait_recv()
-        mine[k] = mine[k] + from_pair[k]
         for q in range(1, chips):
-            to_chips[k, q - 1] = mine[k, q * rows:(q + 1) * rows, :].astype(BF16)
-        for q in range(1, chips):
+            lines = slice(q * rows, (q + 1) * rows)
+            to_chips[k, q - 1] = (mine[k, lines, :] + from_pair[k, lines, :]).astype(BF16)
             pltpu.make_async_remote_copy(
                 src_ref=to_chips.at[k, q - 1], dst_ref=from_chips.at[k, q - 1],
                 send_sem=zs_sem.at[k], recv_sem=zr_sem.at[k],
@@ -162,9 +161,7 @@
 
     for k in range(PARTS):
         produce(k)
-        if k > 0:
-            forward(k - 1)
-    forward(PARTS - 1)
+        forward(k)
 
     for copy in gathers:
         copy.wait_recv()
@@ -175,7 +172,7 @@
 
     for k in range(PARTS):
         pltpu.make_async_copy(from_chips.at[k], from_chips.at[k], zr_sem.at[k]).wait()
-        total = mine[k, 0:rows, :]
+        total = mine[k, 0:rows, :] + from_pair[k, 0:rows, :]
         for q in range(1, chips):
             total = total + from_chips[k, q - 1].astype(F32)
         ig[:, k * piece:(k + 1) * piece] = total.astype(BF16)

time: 15.3 us -> 16.3 us (1.065)
  Pallas kernels: 14.5 us -> 15.5 us
    pallas_call x1, Pallas kernels: 13.7 us -> 14.7 us  [local(): pl.pallas_call(functools.partial(kernel, n_dp, n_t), out_shape=(pltpu.VME...]
where the time goes in v4:
time: 16.3 us; the launch traced here: 16.2 us
  Pallas kernels  15.5 us (95%)
  between operations  0.64 us (4%)
    pallas_call x1, Pallas kernels, local(): pl.pallas_call(functools.partial(kernel, n_dp, n_t), out_shape=(pltpu.VME...  14.7 us
    pallas_call x1, Pallas kernels, local(): pl.pallas_call(place_kernel, out_shape=(jax.ShapeDtypeStruct((rows, width...  0.88 us

profile of v4, /device:TPU:0, one launch (start us, length us, event | category | flops | bytes accessed | tf_op | source)
XLA Modules:
  0.0 16.2 jit_solution(10676726632039688461)
XLA Ops:
  0.6 14.7 %shard_map.77 = (bf16[2,8192]{1,0:T(2,128)(2,1)S(1)}, bf16[176,2048]{1,0:T(8,128)(2,1)S(1)}) custom-call(bf16[16,8192]{1,0:T(8,128)(2,1)} %g_hbm.1, bf16[16,176]{1,0:T(8,128)(2,1)} %gate_hbm.1, bf16[16,176]{1,0:T(8,128)(2,1)} %up_hbm.1, bf16[176,8192]{1,0:T(8,128)(2,1)} %wg_hbm.1, bf16[176,8192]{1,0:T(8,128)(2,1)} %wu_hbm.1, bf16[176,8192]{1,0:T(8,128)(2,1)} %wd_hbm.1), custom_call_target="tpu_custom_call" | custom-call | flops 184549376 | bytes 8650752 | tf_op jit(solution)/shard_map/pallas_call | solution.py:204
  15.3 0.9 %shard_map.78 = (bf16[2,8192]{1,0:T(2,128)(2,1)}, bf16[176,2048]{1,0:T(8,128)(2,1)}) custom-call(bf16[2,8192]{1,0:T(2,128)(2,1)S(1)} %get-tuple-element.4.ig, bf16[176,2048]{1,0:T(8,128)(2,1)S(1)} %get-tuple-element.5.dg), custom_call_target="tpu_custom_call" | custom-call | tf_op jit(solution)/shard_map/pallas_call | solution.py:248
